TPU v7x, 32 devices: a whole 2x2x4 slice. The times are simulated.
32 devices in a mesh: slab: 16 (over z, y, x), grp: 2 (over core).
Axes of the slice: x: 2, y: 2, z: 4, core: 2. Of those that a mesh axis runs over, the one named last changes fastest.
Arguments:
- ply_masks: int32 [3, 32768], P(None, ('slab', 'grp')), may hold values from 0 to 65535, as said below
- severity: bfloat16 [48, 32768], P(None, ('slab', 'grp')), may hold values from 0.29882812 to 0.8984375
- shape_grads: float32 [8, 32768], P(None, ('slab', 'grp')), may hold values from -4 to 4
- element_area: float32 [32768], P(('slab', 'grp')), may hold values from 0.5 to 2
- displacement: float32 [24, 32768], P(None, ('slab', 'grp')), may hold values from -6 to 6
- ply_stiffness: float32 [8, 48], replicated
- live_counts: int32 [32], P(('slab', 'grp')), may hold values from 1 to 1024, as said below
- connectivity: int32 [4, 32768], P(None, ('slab', 'grp')), may hold values from 0 to 1279, as said below
- interface_slots: int32 [2, 4096], P(None, ('slab', 'grp')), may hold values from 0 to 1023, as said below
- send_rows: int32 [4096], P(('slab', 'grp')), may hold values from 0 to 1023
- seam_rows: int32 [4096], P(('slab', 'grp')), may hold values from 0 to 1023
Outputs:
- assembled: float32 [42, 32768], P(None, ('slab', 'grp'))
Inputs may be any that keep to these rules, and one draw needn't show every extreme that they name: `ply_masks`: bit j of word w is the damaged state of ply 16 w + j; the share of damaged plies differs from device to device. `live_counts`: A device uses its element slots 0 up to its count minus one; one device uses all of them. `connectivity`: values are local slots of the element's own device. `interface_slots`: on each device the 256 entries of both lists are distinct element slots.
All inputs are finite; a program needn't handle non-finite values.
Results may differ from a plain program's by a relative error of at most 0.0003.
Values may be sent and summed in bfloat16 or wider, within the bound.
A program may use at most 128 MiB of HBM per device.

v0:
```python
import jax
import jax.numpy as jnp
from jax import lax
from jax.sharding import PartitionSpec as P

drill_factor = 0.1
shear_factor = 5.0 / 6.0


def padded(value, sides, width):
    for axis, dim in sides:
        size, length = (lax.axis_size(axis), value.shape[dim])
        up = [(i, (i + 1) % size) for i in range(size - 1)]
        down = [(j, i) for i, j in up]
        last = lax.slice_in_dim(value, length - width, length, axis=dim)
        first = lax.slice_in_dim(value, 0, width, axis=dim)
        before = lax.ppermute(last, axis, up)
        after = lax.ppermute(first, axis, down)
        value = jnp.concatenate([before, value, after], axis=dim)
    return value


def shifted(block, axis, distance):
    devices = range(lax.axis_size(axis))
    route = [((i - distance) % len(devices), i) for i in devices]
    return lax.ppermute(block, axis, route)


def damage_values(ply_masks, severity):
    powers = 2 ** jnp.arange(16, dtype=jnp.int32)
    ply_bits = ply_masks[:, None, :] // powers[None, :, None] % 2
    ply_bits = ply_bits.reshape(48, -1)
    return ply_bits.astype(jnp.float32) * severity.astype(jnp.float32)


def ply_table(ply_stiffness):
    ply_count = ply_stiffness.shape[1]
    thickness = 1.0 / ply_count
    centre = -0.5 + thickness * (jnp.arange(ply_count, dtype=jnp.float32) + 0.5)
    moment_zero = thickness * jnp.ones_like(centre)
    moment_one = thickness * centre
    moment_two = thickness * centre * centre + thickness**3 / 12.0
    pieces = [
        ply_stiffness[0:6] * moment_zero[None],
        ply_stiffness[0:6] * moment_one[None],
        ply_stiffness[0:6] * moment_two[None],
        ply_stiffness[6:8] * (shear_factor * moment_zero)[None],
    ]
    return jnp.concatenate(pieces, axis=0)


def symmetric(c):
    return [[c[0], c[1], c[2]], [c[1], c[3], c[4]], [c[2], c[4], c[5]]]


def stiffness(laminate):
    nothing = jnp.zeros_like(laminate[0])
    membrane = symmetric(laminate[0:6])
    coupling = symmetric(laminate[6:12])
    bending = symmetric(laminate[12:18])
    matrix_rows = []
    for i in range(3):
        matrix_rows.append(membrane[i] + coupling[i] + [nothing] * 3)
    for i in range(3):
        matrix_rows.append(coupling[i] + bending[i] + [nothing] * 3)
    matrix_rows.append([nothing] * 6 + [laminate[19], nothing, nothing])
    matrix_rows.append([nothing] * 6 + [nothing, laminate[18], nothing])
    matrix_rows.append([nothing] * 8 + [drill_factor * laminate[5]])
    return jnp.stack([jnp.stack(r, 0) for r in matrix_rows], 0)


def strain_map(shape_grads):
    nothing = jnp.zeros_like(shape_grads[0])
    quarter = 0.25 * jnp.ones_like(shape_grads[0])
    corners = []
    for node in range(4):
        grad_x = shape_grads[2 * node]
        grad_y = shape_grads[2 * node + 1]
        matrix_rows = [
            [grad_x, nothing, nothing, nothing, nothing, nothing],
            [nothing, grad_y, nothing, nothing, nothing, nothing],
            [grad_y, grad_x, nothing, nothing, nothing, nothing],
            [nothing, nothing, nothing, nothing, grad_x, nothing],
            [nothing, nothing, nothing, -grad_y, nothing, nothing],
            [nothing, nothing, nothing, -grad_x, grad_y, nothing],
            [nothing, nothing, grad_x, nothing, quarter, nothing],
            [nothing, nothing, grad_y, -quarter, nothing, nothing],
            [0.5 * grad_y, -0.5 * grad_x, nothing, nothing, nothing, quarter],
        ]
        corners.append(jnp.stack([jnp.stack(r, 0) for r in matrix_rows], 0))
    return jnp.stack(corners, 0)


def element_terms(factors, shape_grads, element_area, displacement, ply_weights):
    highest = lax.Precision.HIGHEST
    n = factors.shape[1]
    laminate = jnp.dot(ply_weights, factors, precision=highest, preferred_element_type=jnp.float32)
    constitutive = stiffness(laminate)
    mapping = strain_map(shape_grads)
    strain = jnp.einsum("aijn,ajn->in", mapping, displacement.reshape(4, 6, n), precision=highest)
    stress = jnp.einsum("ijn,jn->in", constitutive, strain, precision=highest)
    nodal_force = element_area[None, None] * jnp.einsum(
        "aijn,in->ajn", mapping, stress, precision=highest
    )
    stiff_map = jnp.einsum("ijn,ajkn->aikn", constitutive, mapping, precision=highest)
    blocks = element_area[None, None, None] * jnp.einsum(
        "aijn,aikn->ajkn", mapping, stiff_map, precision=highest
    )
    return jnp.concatenate([blocks.reshape(4, 36, n), nodal_force], axis=1).reshape(168, n)


def local_terms(packed, live_count, ply_weights):
    ply_count = ply_weights.shape[1]
    local_count = packed.shape[1]
    block_width = 256
    column = jnp.arange(block_width, dtype=jnp.int32)

    def one_block(index, accumulated):
        start = index * block_width
        block_data = lax.dynamic_slice_in_dim(packed, start, block_width, 1)
        element_rows = element_terms(
            block_data[:ply_count],
            block_data[ply_count : ply_count + 8],
            block_data[ply_count + 8],
            block_data[ply_count + 9 : ply_count + 33],
            ply_weights,
        )
        element_rows = jnp.where((start + column)[None] < live_count, element_rows, 0.0)
        return lax.dynamic_update_slice_in_dim(accumulated, element_rows, start, 1)

    blocks = (live_count + block_width - 1) // block_width
    return lax.fori_loop(0, blocks, one_block, jnp.zeros((168, local_count), jnp.float32))


def on_device(
    ply_masks,
    severity,
    shape_grads,
    element_area,
    displacement,
    ply_stiffness,
    live_counts,
    connectivity,
    interface_slots,
    send_rows,
    seam_rows,
):
    local_count = ply_masks.shape[1]
    damage = damage_values(ply_masks, severity)
    chosen = jnp.stack(
        [damage[:, interface_slots[0]], damage[:, interface_slots[1]]], axis=1
    ).astype(jnp.bfloat16)
    rimmed = padded(chosen, (("slab", 1),), 1)
    from_prev = rimmed[:, 0].astype(jnp.float32)
    from_next = rimmed[:, 3].astype(jnp.float32)
    settled = damage.at[:, interface_slots[0]].set(
        0.5 * (damage[:, interface_slots[0]] + from_prev)
    )
    settled = settled.at[:, interface_slots[1]].set(
        0.5 * (damage[:, interface_slots[1]] + from_next)
    )
    factors = 1.0 - settled
    ply_weights = ply_table(ply_stiffness)
    live_count = live_counts[0]
    packed = jnp.concatenate([factors, shape_grads, element_area[None], displacement], axis=0)
    nodal_terms = local_terms(packed, live_count, ply_weights)
    slab_count = lax.axis_size("slab")
    capacity = send_rows.shape[0] // slab_count
    seam_width = seam_rows.shape[0]
    shared_end = local_count + slab_count * capacity
    row_values = (
        nodal_terms.reshape(4, 42, local_count).transpose(1, 0, 2).reshape(42, 4 * local_count)
    )
    slot_sums = (
        jnp.zeros((42, shared_end + seam_width), jnp.float32)
        .at[:, connectivity.reshape(-1)]
        .add(row_values)
    )
    owned_rows = slot_sums[:, :local_count]
    shared = slot_sums[:, local_count:shared_end].reshape(42, slab_count, capacity)
    seam_values = slot_sums[:, shared_end:]
    target_rows = send_rows.reshape(1, slab_count, capacity)
    gathered, gathered_rows = (
        lax.all_gather(shared[None], "slab", axis=0, tiled=True),
        lax.all_gather(target_rows, "slab", axis=0, tiled=True),
    )
    my_index = lax.axis_index("slab")
    picked = lax.dynamic_index_in_dim(gathered, my_index, 2, keepdims=False)
    received_values = picked.transpose(1, 0, 2).reshape(42, slab_count * capacity)
    received_ids = lax.dynamic_index_in_dim(gathered_rows, my_index, 1, keepdims=False).reshape(-1)
    seam_received, seam_ids = shifted((seam_values, seam_rows), "grp", 1)
    assembled = owned_rows.at[:, received_ids].add(received_values)
    return assembled.at[:, seam_ids].add(seam_received)


def solution(mesh):
    in_specs = (
        P(None, ("slab", "grp")),
        P(None, ("slab", "grp")),
        P(None, ("slab", "grp")),
        P(("slab", "grp")),
        P(None, ("slab", "grp")),
        P(),
        P(("slab", "grp")),
        P(None, ("slab", "grp")),
        P(None, ("slab", "grp")),
        P(("slab", "grp")),
        P(("slab", "grp")),
    )
    out_specs = P(None, ("slab", "grp"))
    return jax.shard_map(
        on_device, mesh=mesh, in_specs=in_specs, out_specs=out_specs, check_vma=False
    )
```

profile of v0, /device:TPU:0, one launch (start us, length us, event | category | flops | bytes accessed | tf_op | source)
XLA Modules:
  0.0 235.8 jit_solution(14927123509893804951)
XLA Ops:
  0.1 1.1 copy.57
  1.2 0.7 sign.21
  1.9 0.7 rem.74
  3.3 0.8 fusion.76
  4.0 5.3 %fusion.48 = f32[48,1024]{0,1:T(8,128)S(1)} fusion(bf16[48,1024]{0,1:T(8,128)(2,1)S(1)} %copy.57, s32[48,1024]{0,1:T(8,128)S(1)} %copy.55, s32[48,1024]{0,1:T(8,128)S(1)} %copy.54, s32[48]{0:T(128)S(1)} %rem.77, s32[48]{0:T(128)S(1)} %ne.150), kind=kLoop, calls=%fused_computation.165 | loop fusion | flops 1032192 | bytes 688512 | tf_op jit(solution)/shard_map/mul | solution.py:33
  10.0 4.8 %collective-permute-start = (bf16[48,1,128]{0,2,1:T(8,128)(2,1)S(1)}, bf16[48,1,128]{0,2,1:T(8,128)(2,1)S(1)}, u32[]{:S(2)}, u32[]{:S(2)}) collective-permute-start(bf16[48,1,128]{0,2,1:T(8,128)(2,1)S(1)} %fusion.68), channel_id=1, source_target_pairs={{0,2},{2,4},{4,6},{6,8},{8,10},{10,12},{12,14},{14,16},{16,18},{18... | collective-permute-start | bytes 36872 | tf_op jit(solution)/shard_map/ppermute | solution.py:17
  14.9 0.6 gather_fusion
  15.6 1.3 collective-permute-start.1
  18.1 42.4 %all_gather.6 = s32[16,16,8]{1,2,0:T(8,128)S(1)} all-gather(s32[1,16,8]{1,2,0:T(8,128)S(1)} %copy.64), channel_id=1, replica_groups=mesh['slab'=16,'grp'=2] {'slab'}, dimensions={0}, use_global_device_ids=true | all-gather | bytes 8704 | tf_op jit(solution)/shard_map/all_gather | solution.py:185
  61.6 1.1 scatter_custom_fusion
  62.7 1.1 scatter_custom_fusion.1
  64.6 61.0 %while.11 = (s32[]{:T(128)}, f32[168,1024]{1,0:T(8,128)S(1)}, s32[]{:T(128)}, s32[]{:T(128)}, f32[81,1024]{1,0:T(8,128)S(1)}, /*index=5*/f32[20,48]{1,0:T(8,128)...) while((s32[]{:T(128)}, f32[168,1024]{1,0:T(8,128)S(1)}, ...), condition=%wide.region_3.4_spmd.clone, body=%wide.region_2.3_spmd.clone.sunk | while | flops 14099211 | bytes 9322307 | solution.py:132
  67.0 1.3 copy.102
  68.3 3.4 %fusion.112 = f32[256,1,9]{2,1,0:T(1,128)S(1)} fusion(f32[9,256,1]{0,2,1:T(1,128)S(1)} %bitcast.375, f32[9,9,256]{1,0,2:T(8,128)S(1)} %copy.102), kind=kOutput, calls=%fused_computation.229.clone.1 | convolution fusion | flops 248832 | bytes 101376 | tf_op jit(solution)/shard_map/while/body/ijn,jn->in/dot_general | solution.py:101
  71.9 2.7 %copy.104 = f32[4,9,6,256]{1,2,3,0:T(8,128)} copy(f32[4,9,6,256]{3,2,1,0:T(8,128)S(1)} %pad_maximum_fusion.52) | data formatting | bytes 442368 | tf_op jit(solution)/shard_map/while/body/stack | solution.py:91
  74.6 8.4 %fusion.114 = f32[256,4,6,9]{3,2,0,1:T(8,128)S(1)} fusion(f32[4,9,6,256]{1,2,3,0:T(8,128)} %copy.104, f32[9,9,256]{1,0,2:T(8,128)S(1)} %copy.102), kind=kOutput, calls=%fused_computation.11.clone.1 | convolution fusion | flops 5971968 | bytes 525312 | tf_op jit(solution)/shard_map/while/body/ijn,ajkn->aikn/dot_general | solution.py:105
  83.0 8.6 %multiply_bitcast_fusion.2 = f32[4,6,6,256]{1,2,3,0:T(8,128)} fusion(f32[4,9,6,256]{1,2,3,0:T(8,128)S(1)} %copy-done, f32[256,4,6,9]{3,2,0,1:T(8,128)S(1)} %fusion.114, f32[256]{0:T(256)S(1)} %bitcast.384), kind=kOutput, calls=%fused_computation.10.clone.1 | convolution fusion | flops 4018176 | bytes 590848 | tf_op jit(solution)/shard_map/while/body/aijn,aikn->ajkn/dot_general | solution.py:106
  91.6 2.8 %copy.105 = f32[4,6,6,256]{3,0,2,1:T(4,128)S(1)} copy(f32[4,6,6,256]{1,2,3,0:T(8,128)} %multiply_bitcast_fusion.2) | data formatting | bytes 294912 | tf_op jit(solution)/shard_map/while/body/mul | solution.py:106
  94.4 0.7 fusion.115
  97.3 1.3 copy.102
  98.6 3.4 %fusion.112 = f32[256,1,9]{2,1,0:T(1,128)S(1)} fusion(f32[9,256,1]{0,2,1:T(1,128)S(1)} %bitcast.375, f32[9,9,256]{1,0,2:T(8,128)S(1)} %copy.102), kind=kOutput, calls=%fused_computation.229.clone.1 | convolution fusion | flops 248832 | bytes 101376 | tf_op jit(solution)/shard_map/while/body/ijn,jn->in/dot_general | solution.py:101
  102.2 2.7 %copy.104 = f32[4,9,6,256]{1,2,3,0:T(8,128)} copy(f32[4,9,6,256]{3,2,1,0:T(8,128)S(1)} %pad_maximum_fusion.52) | data formatting | bytes 442368 | tf_op jit(solution)/shard_map/while/body/stack | solution.py:91
  104.9 8.4 %fusion.114 = f32[256,4,6,9]{3,2,0,1:T(8,128)S(1)} fusion(f32[4,9,6,256]{1,2,3,0:T(8,128)} %copy.104, f32[9,9,256]{1,0,2:T(8,128)S(1)} %copy.102), kind=kOutput, calls=%fused_computation.11.clone.1 | convolution fusion | flops 5971968 | bytes 525312 | tf_op jit(solution)/shard_map/while/body/ijn,ajkn->aikn/dot_general | solution.py:105
  113.3 8.6 %multiply_bitcast_fusion.2 = f32[4,6,6,256]{1,2,3,0:T(8,128)} fusion(f32[4,9,6,256]{1,2,3,0:T(8,128)S(1)} %copy-done, f32[256,4,6,9]{3,2,0,1:T(8,128)S(1)} %fusion.114, f32[256]{0:T(256)S(1)} %bitcast.384), kind=kOutput, calls=%fused_computation.10.clone.1 | convolution fusion | flops 4018176 | bytes 590848 | tf_op jit(solution)/shard_map/while/body/aijn,aikn->ajkn/dot_general | solution.py:106
  121.9 2.8 %copy.105 = f32[4,6,6,256]{3,0,2,1:T(4,128)S(1)} copy(f32[4,6,6,256]{1,2,3,0:T(8,128)} %multiply_bitcast_fusion.2) | data formatting | bytes 294912 | tf_op jit(solution)/shard_map/while/body/mul | solution.py:106
  124.8 0.7 fusion.115
  126.8 0.7 copy.63
  127.5 22.5 %scatter_custom_fusion.2 = f32[42,1280]{0,1:T(8,128)S(1)} fusion(s32[4096]{0:T(1024)S(1)} %bitcast.387, f32[4096,42]{1,0:T(8,128)S(1)} %copy.63, f32[]{:T(128)} %constant.51.clone.1), kind=kCustom, calls=%fused_computation.169 | custom fusion | flops 172032 | bytes 215044 | tf_op jit(solution)/shard_map/scatter-add | solution.py:177
  150.1 81.8 %all_gather.7 = f32[16,42,16,8]{1,3,2,0:T(8,128)S(1)} all-gather(f32[1,42,16,8]{1,3,2,0:T(8,128)S(1)} %get-tuple-element.172), channel_id=1, replica_groups=mesh['slab'=16,'grp'=2] {'slab'}, dimensions={0}, use_global_device_ids=true | all-gather | bytes 365568 | tf_op jit(solution)/shard_map/all_gather | solution.py:184
  232.0 1.5 scatter_custom_fusion.3
  233.5 1.5 scatter_custom_fusion.4
  234.9 0.9 copy.65
  (218 shorter events, 9.0 us)
Async XLA Ops:
  0.0 16.9 %copy-start.9 = (s32[128]{0:T(128)S(1)}, s32[128]{0:T(128)}, u32[]{:S(2)}) copy-start(s32[128]{0:T(128)} %param.23) | copy-start | bytes 1540
  0.0 17.6 %copy-start.5 = (s32[4,1024]{1,0:T(4,128)S(1)}, s32[4,1024]{1,0:T(4,128)}, u32[]{:S(2)}) copy-start(s32[4,1024]{1,0:T(4,128)} %param.20) | copy-start | bytes 49156
  0.0 17.7 %copy-start.3 = (f32[24,1024]{1,0:T(8,128)S(1)}, f32[24,1024]{1,0:T(8,128)}, u32[]{:S(2)}) copy-start(f32[24,1024]{1,0:T(8,128)} %param.17) | copy-start | bytes 294916
  0.0 17.9 %copy-start.6 = (f32[8,48]{1,0:T(8,128)S(1)}, f32[8,48]{1,0:T(8,128)}, u32[]{:S(2)}) copy-start(f32[8,48]{1,0:T(8,128)} %param.18) | copy-start | bytes 4612
  0.0 17.9 %copy-start.8 = (s32[128]{0:T(128)S(1)}, s32[128]{0:T(128)}, u32[]{:S(2)}) copy-start(s32[128]{0:T(128)} %param.22) | copy-start | bytes 1540
  0.0 61.1 %copy-start.7 = (f32[1024]{0:T(1024)S(1)}, f32[1024]{0:T(1024)}, u32[]{:S(2)}) copy-start(f32[1024]{0:T(1024)} %param.16) | copy-start | bytes 12292
  0.0 61.3 %copy-start.4 = (f32[8,1024]{1,0:T(8,128)S(1)}, f32[8,1024]{1,0:T(8,128)}, u32[]{:S(2)}) copy-start(f32[8,1024]{1,0:T(8,128)} %param.15) | copy-start | bytes 98308
  10.0 51.5 %collective-permute-start = (bf16[48,1,128]{0,2,1:T(8,128)(2,1)S(1)}, bf16[48,1,128]{0,2,1:T(8,128)(2,1)S(1)}, u32[]{:S(2)}, u32[]{:S(2)}) collective-permute-start(bf16[48,1,128]{0,2,1:T(8,128)(2,1)S(1)} %fusion.68), channel_id=1, source_target_pairs={{0,2},{2,4},{4,6},{6,8},{8,10},{10,12},{12,14},{14,16},{16,18},{18... | collective-permute-start | bytes 36872 | tf_op jit(solution)/shard_map/ppermute | solution.py:17
  15.6 47.1 %collective-permute-start.1 = (bf16[48,1,128]{0,2,1:T(8,128)(2,1)S(1)}, bf16[48,1,128]{0,2,1:T(8,128)(2,1)S(1)}, u32[]{:S(2)}, u32[]{:S(2)}) collective-permute-start(bf16[48,1,128]{0,2,1:T(8,128)(2,1)S(1)} %fusion.67), channel_id=1, source_target_pairs={{2,0},{4,2},{6,4},{8,6},{10,8},{12,10},{14,12},{16,14},{18,16},{20... | collective-permute-start | bytes 36872 | tf_op jit(solution)/shard_map/ppermute | solution.py:18
  16.9 44.7 %collective-permute-start.2 = (s32[128]{0:T(128)S(1)}, s32[128]{0:T(128)S(1)}, u32[]{:S(2)}, u32[]{:S(2)}) collective-permute-start(s32[128]{0:T(128)S(1)} %copy-done.9), channel_id=1, source_target_pairs={{1,0},{0,1},{3,2},{2,3},{5,4},{4,5},{7,6},{6,7},{9,8},{8,9},{11,10... | collective-permute-start | bytes 1544 | tf_op jit(solution)/shard_map/ppermute | solution.py:26
  64.8 2.1 copy-start.1
  74.6 8.4 %copy-start = (f32[4,9,6,256]{1,2,3,0:T(8,128)S(1)}, f32[4,9,6,256]{1,2,3,0:T(8,128)}, u32[]{:S(2)}) copy-start(f32[4,9,6,256]{1,2,3,0:T(8,128)} %copy.104) | copy-start | bytes 663556 | tf_op jit(solution)/shard_map/while
  91.6 3.6 %copy-start.2 = (f32[81,1024]{1,0:T(8,128)S(1)}, f32[81,1024]{1,0:T(8,128)}, u32[]{:S(2)}) copy-start(f32[81,1024]{1,0:T(8,128)} %copy-done.1) | copy-start | bytes 995332 | tf_op jit(solution)/shard_map/while
  95.2 2.1 copy-start.1
  104.9 8.4 %copy-start = (f32[4,9,6,256]{1,2,3,0:T(8,128)S(1)}, f32[4,9,6,256]{1,2,3,0:T(8,128)}, u32[]{:S(2)}) copy-start(f32[4,9,6,256]{1,2,3,0:T(8,128)} %copy.104) | copy-start | bytes 663556 | tf_op jit(solution)/shard_map/while
  121.9 3.6 %copy-start.2 = (f32[81,1024]{1,0:T(8,128)S(1)}, f32[81,1024]{1,0:T(8,128)}, u32[]{:S(2)}) copy-start(f32[81,1024]{1,0:T(8,128)} %copy-done.1) | copy-start | bytes 995332 | tf_op jit(solution)/shard_map/while
  150.1 83.4 %collective-permute-start.3 = (f32[42,128]{0,1:T(8,128)S(1)}, f32[42,128]{0,1:T(8,128)S(1)}, u32[]{:S(2)}, u32[]{:S(2)}) collective-permute-start(f32[42,128]{0,1:T(8,128)S(1)} %get-tuple-element.171), channel_id=1, source_target_pairs={{1,0},{0,1},{3,2},{2,3},{5,4},{4,5},{7,6},{6,7},{9,8},{8,9},{11,10... | collective-permute-start | bytes 64520 | tf_op jit(solution)/shard_map/ppermute | solution.py:26
where the time goes:
time: 237 us; the launch traced here: 236 us
  blocking collectives  124 us (52%)
  matrix products  41 us (17%)
  other arithmetic  37.6 us (16%)
  local copies, waits for them, and re-layouts  24.3 us (10%)
  starting transfers between devices  6.28 us (3%)
    all_gather x1, blocking collectives, on_device(): lax.all_gather(shared[None], 'slab', axis=0, tiled=True)  81.8 us
    all_gather x1, blocking collectives, on_device(): lax.all_gather(target_rows, 'slab', axis=0, tiled=True)  42.4 us
    scatter-add x1, other arithmetic, on_device(): slot_sums = jnp.zeros((42, shared_end + seam_width), jnp.float32).at[:, c...  22.5 us
    dot_general x2, matrix products, element_terms(): jnp.einsum('aijn,aikn->ajkn', mapping, stiff_map, precision=highest)  17.2 us
    dot_general x2, matrix products, element_terms(): jnp.einsum('ijn,ajkn->aikn', constitutive, mapping, precision=highest)  16.7 us
    dot_general x2, matrix products, element_terms(): stress = jnp.einsum('ijn,jn->in', constitutive, strain, precision=highest)  6.76 us
    mul x2, local copies, waits for them, and re-layouts, element_terms(): element_area[None, None, None]  5.51 us
    another operation x2, local copies, waits for them, and re-layouts, strain_map(): return jnp.stack(corners, 0)  5.46 us
  transfers between devices with their start and end apart: 4, of which 0 were waited for; matrix products, arithmetic and copies ran while one was open for 2% of the time, Pallas kernels for 0%

commit v1 on v0

v1 whole, which is shorter than its diff:
```python
import functools

import jax
import jax.numpy as jnp
from jax import lax
from jax.experimental import pallas as pl
from jax.experimental.pallas import tpu as pltpu
from jax.sharding import PartitionSpec as P

MESH = pl.DeviceIdType.MESH
NT = (((1,), (1,)), ((), ()))
NN = (((1,), (0,)), ((), ()))
ROWS = 24
ID_ROW = 22
LO = 256

PAIRS = {
    (0, 0): 0, (0, 1): 1, (1, 1): 2, (0, 3): 3, (0, 4): 4, (1, 3): 5, (1, 4): 6, (0, 5): 7,
    (1, 5): 8, (2, 2): 9, (2, 3): 10, (2, 4): 11, (3, 3): 12, (3, 4): 13, (4, 4): 14, (5, 5): 15,
}


def dot(a, b, dims):
    return lax.dot_general(a, b, dims, preferred_element_type=jnp.float32)


def pair(x):
    high = x.astype(jnp.bfloat16).astype(jnp.float32)
    return jnp.concatenate([high, x - high], axis=0)


def unpair(x):
    return x[:ROWS] + x[ROWS:]


def symmetric(c, at):
    r = [c[at + i : at + i + 1] for i in range(6)]
    return [[r[0], r[1], r[2]], [r[1], r[3], r[4]], [r[2], r[4], r[5]]]


def kernel(
    n_slab, n_grp, masks_ref, sev_ref, grads_ref, area_ref, disp_ref, stiff_ref, live_ref,
    conn_ref, face_ref, send_rows_ref, seam_rows_ref, out_ref,
    near_out, near_in, vals, spread, send_buf, recv_buf, seam_out, seam_in,
    near_send, near_recv, send_sem, recv_sem, seam_send, seam_recv,
):
    f32, bf16, i32 = jnp.float32, jnp.bfloat16, jnp.int32
    s, g = lax.axis_index("slab"), lax.axis_index("grp")
    n = masks_ref.shape[1]
    cap = send_rows_ref.shape[1] // n_slab
    shared = n_slab * cap
    seam = seam_rows_ref.shape[1]
    plies = sev_ref.shape[0]
    groups = n // LO
    rest = -(-(shared + seam) // LO)
    faces = face_ref.shape[1]
    next_grp = lax.rem(g + 1, n_grp)
    prev_grp = lax.rem(g + n_grp - 1, n_grp)

    barrier = pltpu.get_barrier_semaphore()
    for k in range(1, n_slab):
        pl.semaphore_signal(
            barrier, inc=1, device_id=(lax.rem(s + k, n_slab), g), device_id_type=MESH
        )
    around = (next_grp,) if n_grp == 2 else (next_grp, prev_grp)
    for other in around:
        pl.semaphore_signal(barrier, inc=1, device_id=(s, other), device_id_type=MESH)

    parts = []
    for w in range(plies // 16):
        word = jnp.broadcast_to(masks_ref[w : w + 1, :], (16, n))
        parts.append((word >> lax.broadcasted_iota(i32, (16, n), 0)) & 1)
    damage = jnp.concatenate(parts, axis=0).astype(f32) * sev_ref[...].astype(f32)
    face = jnp.concatenate([face_ref[0:1, :], face_ref[1:2, :]], axis=1)
    onface = (lax.broadcasted_iota(i32, (n, 2 * faces), 0) == face).astype(f32).astype(bf16)
    chosen = dot(damage.astype(bf16), onface, NN).astype(bf16)
    near_out[0] = chosen[:, :faces]
    near_out[1] = chosen[:, faces:]

    pl.semaphore_wait(barrier, n_slab - 1 + len(around))

    to_prev = pltpu.make_async_remote_copy(
        src_ref=near_out.at[0], dst_ref=near_in.at[1], send_sem=near_send.at[0],
        recv_sem=near_recv.at[1], device_id=(lax.max(s - 1, 0), g), device_id_type=MESH,
    )
    to_next = pltpu.make_async_remote_copy(
        src_ref=near_out.at[1], dst_ref=near_in.at[0], send_sem=near_send.at[1],
        recv_sem=near_recv.at[0], device_id=(lax.min(s + 1, n_slab - 1), g), device_id_type=MESH,
    )

    @pl.when(s > 0)
    def _():
        to_prev.start()

    @pl.when(s < n_slab - 1)
    def _():
        to_next.start()

    @pl.when(s == 0)
    def _():
        near_in[0] = jnp.zeros((plies, faces), bf16)

    @pl.when(s == n_slab - 1)
    def _():
        near_in[1] = jnp.zeros((plies, faces), bf16)

    stiff = stiff_ref[...]
    h = 1.0 / plies
    z = -0.5 + h * (lax.broadcasted_iota(i32, (8, plies), 1).astype(f32) + 0.5)
    row8 = lax.broadcasted_iota(i32, (8, plies), 0)
    weights = jnp.concatenate(
        [
            stiff * jnp.where(row8 < 6, h, 5.0 / 6.0 * h),
            stiff * (h * z),
            stiff * (h * z * z + h**3 / 12.0),
        ],
        axis=0,
    )
    w1 = weights.astype(bf16).astype(f32)
    w2 = (weights - w1).astype(bf16).astype(f32)
    w3 = weights - w1 - w2
    wcat = jnp.concatenate([w1, w2, w3], axis=0).astype(bf16)
    total = jnp.sum(weights, axis=1, keepdims=True)
    facing = dot(jnp.ones((16, 2 * faces), bf16), onface, NT)[0:1]
    own = dot(wcat, (damage * (1.0 - 0.5 * facing)).astype(bf16), NN)
    own = total - (own[0:24] + own[24:48] + own[48:72])

    low_row = lax.broadcasted_iota(i32, (LO, n), 0)
    for a in range(4):
        low = conn_ref[a : a + 1, :] & (LO - 1)
        spread[a] = (low_row == low).astype(f32).astype(bf16)

    def corners(ref, first, step):
        return jnp.concatenate([ref[first + step * a : first + step * a + 1, :] for a in range(4)], axis=0)

    gx, gy = corners(grads_ref, 0, 2), corners(grads_ref, 1, 2)
    u, v, w, tx, ty, tz = [corners(disp_ref, i, 6) for i in range(6)]
    strain = [
        jnp.sum(t, axis=0, keepdims=True)
        for t in (
            gx * u, gy * v, gy * u + gx * v, gx * ty, -gy * tx, gy * ty - gx * tx,
            gx * w + 0.25 * ty, gy * w - 0.25 * tx, 0.25 * tz - 0.5 * (gx * v - gy * u),
        )
    ]
    column = lax.broadcasted_iota(i32, (1, n), 1)
    area = jnp.where(column < live_ref[0], area_ref[...], 0.0)

    @pl.when(s > 0)
    def _():
        to_prev.wait_send()
        to_next.wait_recv()

    @pl.when(s < n_slab - 1)
    def _():
        to_next.wait_send()
        to_prev.wait_recv()

    partner = jnp.concatenate([near_in[0], near_in[1]], axis=1)
    partner = 0.5 * dot(partner, onface, NT)
    other = dot(wcat, partner.astype(bf16), NN)
    lam = area * (own - (other[0:24] + other[24:48] + other[48:72]))

    A, B, D = symmetric(lam, 0), symmetric(lam, 8), symmetric(lam, 16)
    sx, sy, sd = lam[7:8], lam[6:7], 0.1 * lam[5:6]
    e = strain
    stress = [A[i][0] * e[0] + A[i][1] * e[1] + A[i][2] * e[2]
              + B[i][0] * e[3] + B[i][1] * e[4] + B[i][2] * e[5] for i in range(3)]
    stress += [B[i][0] * e[0] + B[i][1] * e[1] + B[i][2] * e[2]
               + D[i][0] * e[3] + D[i][1] * e[4] + D[i][2] * e[5] for i in range(3)]
    stress += [sx * e[6], sy * e[7], sd * e[8]]

    def along_u(m):
        return [m[i][0] * gx + m[i][2] * gy for i in range(3)]

    def along_v(m):
        return [m[i][1] * gy + m[i][2] * gx for i in range(3)]

    au, av, bu, bv, du, dv = along_u(A), along_v(A), along_u(B), along_v(B), along_u(D), along_v(D)
    t = stress
    values = [
        gx * au[0] + gy * au[2] + 0.25 * gy * gy * sd,
        gy * au[1] + gx * au[2] - 0.25 * gx * gy * sd,
        gy * av[1] + gx * av[2] + 0.25 * gx * gx * sd,
        -(gy * bu[1] + gx * bu[2]),
        gx * bu[0] + gy * bu[2],
        -(gy * bv[1] + gx * bv[2]),
        gx * bv[0] + gy * bv[2],
        0.125 * gy * sd,
        -0.125 * gx * sd,
        gx * gx * sx + gy * gy * sy,
        -0.25 * gy * sy,
        0.25 * gx * sx,
        gy * dv[1] + gx * dv[2] + 0.0625 * sy,
        -(gx * dv[0] + gy * dv[2]),
        gx * du[0] + gy * du[2] + 0.0625 * sx,
        jnp.broadcast_to(0.0625 * sd, gx.shape),
        gx * t[0] + gy * t[2] + 0.5 * gy * t[8],
        gy * t[1] + gx * t[2] - 0.5 * gx * t[8],
        gx * t[6] + gy * t[7],
        -gy * t[4] - gx * t[5] - 0.25 * t[7],
        gx * t[3] + gy * t[5] + 0.25 * t[6],
        jnp.broadcast_to(0.25 * t[8], gx.shape),
    ]
    nothing = jnp.zeros_like(gx)
    for i, value in enumerate(values + [nothing] * (ROWS - len(values))):
        for a in range(4):
            vals[a, i : i + 1, :] = value[a : a + 1]

    def scattered(first, count):
        total = None
        for a in range(4):
            both = pair(vals[a])
            group = conn_ref[a : a + 1, :] >> 8
            chosen = jnp.concatenate(
                [jnp.where(group == first + i, both, 0.0) for i in range(count)], axis=0
            ).astype(bf16)
            term = dot(chosen, spread[a], NT)
            total = term if total is None else total + term
        return jnp.concatenate(
            [unpair(total[2 * ROWS * i : 2 * ROWS * (i + 1)]) for i in range(count)], axis=1
        )

    sums = scattered(groups, rest)
    row_of = lax.broadcasted_iota(i32, (ROWS, 128), 0)
    for b in range(shared // 128):
        ids = send_rows_ref[:, 128 * b : 128 * (b + 1)].astype(f32)
        block = jnp.where(row_of == ID_ROW, ids, sums[:, 128 * b : 128 * (b + 1)])
        block = jnp.concatenate([block, jnp.zeros((128 - ROWS, 128), f32)], axis=0).T
        send_buf[pl.ds(b * (128 // cap), 128 // cap)] = block.reshape(128 // cap, cap, 128)
    copies = []
    for k in range(1, n_slab):
        to = lax.rem(s + k, n_slab)
        copies.append(
            pltpu.make_async_remote_copy(
                src_ref=send_buf.at[to], dst_ref=recv_buf.at[s], send_sem=send_sem.at[k],
                recv_sem=recv_sem.at[k], device_id=(to, g), device_id_type=MESH,
            )
        )
        copies[-1].start()
    seam_out[...] = jnp.where(
        row_of == ID_ROW, seam_rows_ref[...].astype(f32), sums[:, shared : shared + seam]
    )
    copies.append(
        pltpu.make_async_remote_copy(
            src_ref=seam_out, dst_ref=seam_in, send_sem=seam_send, recv_sem=seam_recv,
            device_id=(s, next_grp), device_id_type=MESH,
        )
    )
    copies[-1].start()
    recv_buf[s] = send_buf[s]

    owned = scattered(0, groups)

    for copy in copies:
        copy.wait()

    row_lane = lax.broadcasted_iota(i32, (128, n), 1)
    for b in range(shared // 128 + 1):
        if b < shared // 128:
            across = recv_buf[pl.ds(b * (128 // cap), 128 // cap)].reshape(128, 128)
            block = across.T[:ROWS]
        else:
            block = seam_in[...]
            across = jnp.concatenate([block, jnp.zeros((128 - ROWS, 128), f32)], axis=0).T
        ids = across[:, ID_ROW : ID_ROW + 1].astype(i32)
        onto = (row_lane == ids).astype(f32).astype(bf16)
        owned = owned + unpair(dot(pair(block).astype(bf16), onto, NN))

    zero = jnp.zeros((1, n), f32)
    for j in range(6):
        for k in range(6):
            at = PAIRS.get((min(j, k), max(j, k)))
            row = 6 * j + k
            out_ref[row : row + 1, :] = zero if at is None else owned[at : at + 1]
    for j in range(6):
        out_ref[36 + j : 37 + j, :] = owned[16 + j : 17 + j]


def on_device(
    n_slab, n_grp, ply_masks, severity, shape_grads, element_area, displacement, ply_stiffness,
    live_counts, connectivity, interface_slots, send_rows, seam_rows,
):
    f32, bf16 = jnp.float32, jnp.bfloat16
    n = ply_masks.shape[1]
    plies = severity.shape[0]
    cap = send_rows.shape[0] // n_slab
    faces = interface_slots.shape[1]
    seam = seam_rows.shape[0]
    vmem = pl.BlockSpec(memory_space=pltpu.VMEM)
    smem = pl.BlockSpec(memory_space=pltpu.SMEM)
    return pl.pallas_call(
        functools.partial(kernel, n_slab, n_grp),
        out_shape=jax.ShapeDtypeStruct((42, n), f32),
        in_specs=[vmem] * 6 + [smem] + [vmem] * 4,
        out_specs=vmem,
        scratch_shapes=[
            pltpu.VMEM((2, plies, faces), bf16),
            pltpu.VMEM((2, plies, faces), bf16),
            pltpu.VMEM((4, ROWS, n), f32),
            pltpu.VMEM((4, LO, n), bf16),
            pltpu.VMEM((n_slab, cap, 128), f32),
            pltpu.VMEM((n_slab, cap, 128), f32),
            pltpu.VMEM((ROWS, seam), f32),
            pltpu.VMEM((ROWS, seam), f32),
            pltpu.SemaphoreType.DMA((2,)),
            pltpu.SemaphoreType.DMA((2,)),
            pltpu.SemaphoreType.DMA((n_slab,)),
            pltpu.SemaphoreType.DMA((n_slab,)),
            pltpu.SemaphoreType.DMA,
            pltpu.SemaphoreType.DMA,
        ],
        compiler_params=pltpu.CompilerParams(
            collective_id=0, has_side_effects=True, vmem_limit_bytes=40 * 1024 * 1024
        ),
    )(
        ply_masks, severity, shape_grads, element_area[None], displacement, ply_stiffness,
        live_counts, connectivity, interface_slots, send_rows[None], seam_rows[None],
    )


def solution(mesh):
    both = ("slab", "grp")
    in_specs = (
        P(None, both), P(None, both), P(None, both), P(both), P(None, both), P(), P(both),
        P(None, both), P(None, both), P(both), P(both),
    )
    return jax.shard_map(
        functools.partial(on_device, mesh.shape["slab"], mesh.shape["grp"]),
        mesh=mesh, in_specs=in_specs, out_specs=P(None, both), check_vma=False,
    )
```

time: 237 us -> 23.2 us (0.10)
  blocking collectives: 124 us -> 0 us
  matrix products: 41 us -> 0 us
  other arithmetic: 37.6 us -> 0 us
  local copies, waits for them, and re-layouts: 24.3 us -> 6.01 us
  Pallas kernels: 0 us -> 16 us
  starting transfers between devices: 6.28 us -> 0 us
    all_gather x2 -> x0, blocking collectives: 124 us -> none  [the longest x1 81.8 us: on_device(): lax.all_gather(shared[None], 'slab', axis=0, tiled=True)]
    dot_general x8 -> x0, matrix products: 41 us -> none  [the longest x2 17.2 us: element_terms(): jnp.einsum('aijn,aikn->ajkn', mapping, stiff_map, precision=highest)]
    scatter-add x3 -> x0, other arithmetic: 25.5 us -> none  [the longest x1 22.5 us: on_device(): slot_sums = jnp.zeros((42, shared_end + seam_width), jnp.float32).at[:, c...]
    pallas_call x0 -> x1, Pallas kernels: none -> 16 us  [on_device(): pl.pallas_call(functools.partial(kernel, n_slab, n_grp), out_shape=jax.Sh...]
    another operation x58 -> x0, local copies, waits for them, and re-layouts: 9.9 us -> none  [the longest x2 5.46 us: strain_map(): return jnp.stack(corners, 0)]
    ppermute x4 -> x0, starting transfers between devices: 6.28 us -> none  [the longest x1 4.84 us: padded(): before = lax.ppermute(last, axis, up)]
    mul x9 -> x0, other arithmetic: 5.63 us -> none  [the longest x1 5.34 us: damage_values(): return ply_bits.astype(jnp.float32) * severity.astype(jnp.float32)]
    mul x2 -> x0, local copies, waits for them, and re-layouts: 5.51 us -> none  [element_terms(): element_area[None, None, None]]
  transfers between devices with their start and end apart: 4 -> 0, of which waited for: 0 -> 0; matrix products, arithmetic and copies ran while one was open for 2% -> 0% of each run, Pallas kernels for 0% -> 0%
where the time goes in v1:
time: 23.2 us; the launch traced here: 22.8 us
  Pallas kernels  16 us (69%)
  local copies, waits for them, and re-layouts  6.01 us (26%)
  between operations  0.71 us (3%)
    pallas_call x1, Pallas kernels, on_device(): pl.pallas_call(functools.partial(kernel, n_slab, n_grp), out_shape=jax.Sh...  16 us
    unnamed x21, local copies, waits for them, and re-layouts  6.01 us

profile of v1, /device:TPU:0, one launch (start us, length us, event | category | flops | bytes accessed | tf_op | source)
XLA Modules:
  0.0 22.8 jit_solution(17180412779862377542)
XLA Ops:
  0.0 0.0 copy-start.5
  0.7 0.0 copy-start.9
  0.7 0.0 copy-start.7
  0.7 0.0 copy-start.8
  0.7 0.0 copy-done.5
  0.7 0.6 %copy-done.9 = s32[128]{0:T(128)S(1)} copy-done((s32[128]{0:T(128)S(1)}, s32[128]{0:T(128)}, u32[]{:S(2)}) %copy-start.9) | copy-done | bytes 536
  1.3 0.0 copy-done.7
  1.4 0.0 copy-done.8
  1.4 0.0 copy-start
  1.4 0.9 %copy-done = bf16[48,1024]{1,0:T(8,128)(2,1)S(1)} copy-done((bf16[48,1024]{1,0:T(8,128)(2,1)S(1)}, bf16[48,1024]{1,0:T(8,128)(2,1)}, u32[]{:S(2)}) %copy-start) | copy-done | bytes 98328
  2.3 0.0 copy-start.1
  2.3 0.9 %copy-done.1 = f32[24,1024]{1,0:T(8,128)S(1)} copy-done((f32[24,1024]{1,0:T(8,128)S(1)}, f32[24,1024]{1,0:T(8,128)}, u32[]{:S(2)}) %copy-start.1) | copy-done | bytes 98328
  3.2 0.0 copy-start.2
  3.2 0.8 %copy-done.2 = f32[8,1024]{1,0:T(8,128)S(1)} copy-done((f32[8,1024]{1,0:T(8,128)S(1)}, f32[8,1024]{1,0:T(8,128)}, u32[]{:S(2)}) %copy-start.2) | copy-done | bytes 32792
  3.9 0.0 copy-start.3
  3.9 0.7 %copy-done.3 = s32[3,1024]{1,0:T(4,128)S(1)} copy-done((s32[3,1024]{1,0:T(4,128)S(1)}, s32[3,1024]{1,0:T(4,128)}, u32[]{:S(2)}) %copy-start.3) | copy-done | bytes 12312
  4.6 0.0 copy-start.4
  4.6 0.7 %copy-done.4 = s32[4,1024]{1,0:T(4,128)S(1)} copy-done((s32[4,1024]{1,0:T(4,128)S(1)}, s32[4,1024]{1,0:T(4,128)}, u32[]{:S(2)}) %copy-start.4) | copy-done | bytes 16408
  5.3 0.0 copy-start.6
  5.3 0.7 %copy-done.6 = f32[8,48]{1,0:T(8,128)S(1)} copy-done((f32[8,48]{1,0:T(8,128)S(1)}, f32[8,48]{1,0:T(8,128)}, u32[]{:S(2)}) %copy-start.6) | copy-done | bytes 1560
  6.0 16.0 %shard_map.109 = f32[42,1024]{1,0:T(8,128)S(1)} custom-call(s32[3,1024]{1,0:T(4,128)S(1)} %copy-done.3, bf16[48,1024]{1,0:T(8,128)(2,1)S(1)} %copy-done, f32[8,1024]{1,0:T(8,128)S(1)} %copy-done.2, f32[1,1024]{1,0:T(1,128)S(1)} %bitcast.3, f32[24,1024]{1,0:T(8,128)S(1)} %copy-done.1, f32[8,48]{1,0:T(8,128)S(1)} %copy-done.6, s32[1]{0:T(128)S(6)} %copy.13.live_ref, ...), custom_call_target="tpu_custom_call" | custom-call | tf_op jit(solution)/shard_map/pallas_call | solution.py:291
  22.1 0.7 %copy.14 = f32[42,1024]{1,0:T(8,128)} copy(f32[42,1024]{1,0:T(8,128)S(1)} %shard_map.109) | data formatting | bytes 344064
Async XLA Ops:
  0.0 0.7 %copy-start.5 = (f32[1024]{0:T(1024)S(1)}, f32[1024]{0:T(1024)}, u32[]{:S(2)}) copy-start(f32[1024]{0:T(1024)} %param.14) | copy-start | bytes 12292
  0.7 0.7 %copy-start.9 = (s32[128]{0:T(128)S(1)}, s32[128]{0:T(128)}, u32[]{:S(2)}) copy-start(s32[128]{0:T(128)} %param.21) | copy-start | bytes 1540
  0.7 0.7 %copy-start.7 = (s32[2,128]{1,0:T(2,128)S(1)}, s32[2,128]{1,0:T(2,128)}, u32[]{:S(2)}) copy-start(s32[2,128]{1,0:T(2,128)} %face_ref.1) | copy-start | bytes 3076
  0.7 0.7 %copy-start.8 = (s32[128]{0:T(128)S(1)}, s32[128]{0:T(128)}, u32[]{:S(2)}) copy-start(s32[128]{0:T(128)} %param.20) | copy-start | bytes 1540
  1.4 0.9 %copy-start = (bf16[48,1024]{1,0:T(8,128)(2,1)S(1)}, bf16[48,1024]{1,0:T(8,128)(2,1)}, u32[]{:S(2)}) copy-start(bf16[48,1024]{1,0:T(8,128)(2,1)} %sev_ref.1) | copy-start | bytes 294916
  2.3 0.9 %copy-start.1 = (f32[24,1024]{1,0:T(8,128)S(1)}, f32[24,1024]{1,0:T(8,128)}, u32[]{:S(2)}) copy-start(f32[24,1024]{1,0:T(8,128)} %disp_ref.1) | copy-start | bytes 294916
  3.2 0.8 %copy-start.2 = (f32[8,1024]{1,0:T(8,128)S(1)}, f32[8,1024]{1,0:T(8,128)}, u32[]{:S(2)}) copy-start(f32[8,1024]{1,0:T(8,128)} %grads_ref.1) | copy-start | bytes 98308
  3.9 0.7 %copy-start.3 = (s32[3,1024]{1,0:T(4,128)S(1)}, s32[3,1024]{1,0:T(4,128)}, u32[]{:S(2)}) copy-start(s32[3,1024]{1,0:T(4,128)} %masks_ref.1) | copy-start | bytes 36868
  4.6 0.7 %copy-start.4 = (s32[4,1024]{1,0:T(4,128)S(1)}, s32[4,1024]{1,0:T(4,128)}, u32[]{:S(2)}) copy-start(s32[4,1024]{1,0:T(4,128)} %conn_ref.1) | copy-start | bytes 49156
  5.3 0.7 %copy-start.6 = (f32[8,48]{1,0:T(8,128)S(1)}, f32[8,48]{1,0:T(8,128)}, u32[]{:S(2)}) copy-start(f32[8,48]{1,0:T(8,128)} %stiff_ref.1) | copy-start | bytes 4612

commit v2 on v1

--- a/solution.py
+++ b/solution.py
@@ -39,11 +39,23 @@
 
 
 def kernel(
-    n_slab, n_grp, masks_ref, sev_ref, grads_ref, area_ref, disp_ref, stiff_ref, live_ref,
-    conn_ref, face_ref, send_rows_ref, seam_rows_ref, out_ref,
-    near_out, near_in, vals, spread, send_buf, recv_buf, seam_out, seam_in,
-    near_send, near_recv, send_sem, recv_sem, seam_send, seam_recv,
+    n_slab, n_grp, *refs,
 ):
+    inputs, (out_ref,), held, rest = refs[:11], refs[11:12], list(refs[12:22]), refs[22:]
+    held.insert(6, inputs[6])
+    (
+        masks_ref, sev_ref, grads_ref, area_ref, disp_ref, stiff_ref, live_ref,
+        conn_ref, face_ref, send_rows_ref, seam_rows_ref,
+    ) = held
+    (
+        load_sem,
+        near_out, near_in, vals, spread, send_buf, recv_buf, seam_out, seam_in,
+        near_send, near_recv, send_sem, recv_sem, seam_send, seam_recv,
+    ) = rest
+    loads = {}
+    for i in (0, 1, 8, 2, 4, 5, 7, 3, 9, 10):
+        loads[i] = pltpu.make_async_copy(inputs[i], held[i], load_sem.at[i])
+        loads[i].start()
     f32, bf16, i32 = jnp.float32, jnp.bfloat16, jnp.int32
     s, g = lax.axis_index("slab"), lax.axis_index("grp")
     n = masks_ref.shape[1]
@@ -52,7 +64,7 @@
     seam = seam_rows_ref.shape[1]
     plies = sev_ref.shape[0]
     groups = n // LO
-    rest = -(-(shared + seam) // LO)
+    beyond = -(-(shared + seam) // LO)
     faces = face_ref.shape[1]
     next_grp = lax.rem(g + 1, n_grp)
     prev_grp = lax.rem(g + n_grp - 1, n_grp)
@@ -65,6 +77,9 @@
     around = (next_grp,) if n_grp == 2 else (next_grp, prev_grp)
     for other in around:
         pl.semaphore_signal(barrier, inc=1, device_id=(s, other), device_id_type=MESH)
+
+    for i in (0, 1, 8):
+        loads[i].wait()
 
     parts = []
     for w in range(plies // 16):
@@ -103,6 +118,9 @@
     @pl.when(s == n_slab - 1)
     def _():
         near_in[1] = jnp.zeros((plies, faces), bf16)
+
+    for i in (2, 3, 4, 5, 7, 9, 10):
+        loads[i].wait()
 
     stiff = stiff_ref[...]
     h = 1.0 / plies
@@ -220,7 +238,7 @@
             [unpair(total[2 * ROWS * i : 2 * ROWS * (i + 1)]) for i in range(count)], axis=1
         )
 
-    sums = scattered(groups, rest)
+    sums = scattered(groups, beyond)
     row_of = lax.broadcasted_iota(i32, (ROWS, 128), 0)
     for b in range(shared // 128):
         ids = send_rows_ref[:, 128 * b : 128 * (b + 1)].astype(f32)
@@ -286,14 +304,20 @@
     cap = send_rows.shape[0] // n_slab
     faces = interface_slots.shape[1]
     seam = seam_rows.shape[0]
-    vmem = pl.BlockSpec(memory_space=pltpu.VMEM)
-    smem = pl.BlockSpec(memory_space=pltpu.SMEM)
+    arrays = (
+        ply_masks, severity, shape_grads, element_area[None], displacement, ply_stiffness,
+        live_counts, connectivity, interface_slots, send_rows[None], seam_rows[None],
+    )
+    hbm = pl.BlockSpec(memory_space=pltpu.HBM)
+    held = [pltpu.VMEM(a.shape, a.dtype) for a in arrays]
+    held = held[:6] + held[7:]
     return pl.pallas_call(
         functools.partial(kernel, n_slab, n_grp),
         out_shape=jax.ShapeDtypeStruct((42, n), f32),
-        in_specs=[vmem] * 6 + [smem] + [vmem] * 4,
-        out_specs=vmem,
-        scratch_shapes=[
+        in_specs=[hbm] * 6 + [pl.BlockSpec(memory_space=pltpu.SMEM)] + [hbm] * 4,
+        out_specs=pl.BlockSpec(memory_space=pltpu.VMEM),
+        scratch_shapes=held + [
+            pltpu.SemaphoreType.DMA((len(arrays),)),
             pltpu.VMEM((2, plies, faces), bf16),
             pltpu.VMEM((2, plies, faces), bf16),
             pltpu.VMEM((4, ROWS, n), f32),
@@ -310,12 +334,9 @@
             pltpu.SemaphoreType.DMA,
         ],
         compiler_params=pltpu.CompilerParams(
-            collective_id=0, has_side_effects=True, vmem_limit_bytes=40 * 1024 * 1024
+            collective_id=0, has_side_effects=True, vmem_limit_bytes=64 * 1024 * 1024
         ),
-    )(
-        ply_masks, severity, shape_grads, element_area[None], displacement, ply_stiffness,
-        live_counts, connectivity, interface_slots, send_rows[None], seam_rows[None],
-    )
+    )(*arrays)
 
 
 def solution(mesh):

time: 23.2 us -> 19.4 us (0.84)
  local copies, waits for them, and re-layouts: 6.01 us -> 1.62 us
  Pallas kernels: 16 us -> 16.9 us
    unnamed x21 -> x1, local copies, waits for them, and re-layouts: 6.01 us -> 1.62 us
    pallas_call x1, Pallas kernels: 16 us -> 16.9 us  [on_device(): pl.pallas_call(functools.partial(kernel, n_slab, n_grp), out_shape=jax.Sh...]
where the time goes in v2:
time: 19.4 us; the launch traced here: 19.2 us
  Pallas kernels  16.9 us (87%)
  local copies, waits for them, and re-layouts  1.62 us (8%)
  between operations  0.66 us (3%)
    pallas_call x1, Pallas kernels, on_device(): pl.pallas_call(functools.partial(kernel, n_slab, n_grp), out_shape=jax.Sh...  16.9 us
    unnamed x1, local copies, waits for them, and re-layouts  1.62 us

profile of v2, /device:TPU:0, one launch (start us, length us, event | category | flops | bytes accessed | tf_op | source)
XLA Modules:
  0.0 19.2 jit_solution(11925447005990209076)
XLA Ops:
  0.7 16.9 %shard_map.109 = f32[42,1024]{1,0:T(8,128)} custom-call(s32[3,1024]{1,0:T(4,128)} %refs_0_.1, bf16[48,1024]{1,0:T(8,128)(2,1)} %refs_1_.1, f32[8,1024]{1,0:T(8,128)} %refs_2_.1, f32[1,1024]{1,0:T(1,128)} %bitcast.3, f32[24,1024]{1,0:T(8,128)} %refs_4_.1, f32[8,48]{1,0:T(8,128)} %refs_5_.1, s32[1]{0:T(128)S(6)} %copy.13.refs_6_, s32[4,1024]{1,0:T(4,128)} %refs_7_.1, ...), custom_call_target="tpu_custom_call" | custom-call | tf_op jit(solution)/shard_map/pallas_call | solution.py:314
  17.5 1.6 %copy.14 = f32[42,1024]{1,0:T(8,128)} copy(f32[42,1024]{1,0:T(8,128)} %shard_map.109) | data formatting | bytes 344064

commit v3 on v2

v3 whole, which is shorter than its diff:
```python
import functools

import jax
import jax.numpy as jnp
from jax import lax
from jax.experimental import pallas as pl
from jax.experimental.pallas import tpu as pltpu
from jax.sharding import PartitionSpec as P

MESH = pl.DeviceIdType.MESH
NT = (((1,), (1,)), ((), ()))
NN = (((1,), (0,)), ((), ()))
ROWS = 24
ID_ROW = 22
LO = 256

PAIRS = {
    (0, 0): 0, (0, 1): 1, (1, 1): 2, (0, 3): 3, (0, 4): 4, (1, 3): 5, (1, 4): 6, (0, 5): 7,
    (1, 5): 8, (2, 2): 9, (2, 3): 10, (2, 4): 11, (3, 3): 12, (3, 4): 13, (4, 4): 14, (5, 5): 15,
}


def dot(a, b, dims):
    return lax.dot_general(a, b, dims, preferred_element_type=jnp.float32)


def pair(x):
    high = x.astype(jnp.bfloat16).astype(jnp.float32)
    return jnp.concatenate([high, x - high], axis=0)


def unpair(x):
    return x[:ROWS] + x[ROWS:]


def symmetric(c, at):
    r = [c[at + i : at + i + 1] for i in range(6)]
    return [[r[0], r[1], r[2]], [r[1], r[3], r[4]], [r[2], r[4], r[5]]]


def fill(vals, gx, gy, strain, lam):
    A, B, D = symmetric(lam, 0), symmetric(lam, 8), symmetric(lam, 16)
    sx, sy, sd = lam[7:8], lam[6:7], 0.1 * lam[5:6]
    e = strain
    stress = [A[i][0] * e[0] + A[i][1] * e[1] + A[i][2] * e[2]
              + B[i][0] * e[3] + B[i][1] * e[4] + B[i][2] * e[5] for i in range(3)]
    stress += [B[i][0] * e[0] + B[i][1] * e[1] + B[i][2] * e[2]
               + D[i][0] * e[3] + D[i][1] * e[4] + D[i][2] * e[5] for i in range(3)]
    stress += [sx * e[6], sy * e[7], sd * e[8]]

    def along_u(m):
        return [m[i][0] * gx + m[i][2] * gy for i in range(3)]

    def along_v(m):
        return [m[i][1] * gy + m[i][2] * gx for i in range(3)]

    au, av, bu, bv, du, dv = along_u(A), along_v(A), along_u(B), along_v(B), along_u(D), along_v(D)
    t = stress
    values = [
        gx * au[0] + gy * au[2] + 0.25 * gy * gy * sd,
        gy * au[1] + gx * au[2] - 0.25 * gx * gy * sd,
        gy * av[1] + gx * av[2] + 0.25 * gx * gx * sd,
        -(gy * bu[1] + gx * bu[2]),
        gx * bu[0] + gy * bu[2],
        -(gy * bv[1] + gx * bv[2]),
        gx * bv[0] + gy * bv[2],
        0.125 * gy * sd,
        -0.125 * gx * sd,
        gx * gx * sx + gy * gy * sy,
        -0.25 * gy * sy,
        0.25 * gx * sx,
        gy * dv[1] + gx * dv[2] + 0.0625 * sy,
        -(gx * dv[0] + gy * dv[2]),
        gx * du[0] + gy * du[2] + 0.0625 * sx,
        jnp.broadcast_to(0.0625 * sd, gx.shape),
        gx * t[0] + gy * t[2] + 0.5 * gy * t[8],
        gy * t[1] + gx * t[2] - 0.5 * gx * t[8],
        gx * t[6] + gy * t[7],
        -gy * t[4] - gx * t[5] - 0.25 * t[7],
        gx * t[3] + gy * t[5] + 0.25 * t[6],
        jnp.broadcast_to(0.25 * t[8], gx.shape),
    ]
    nothing = jnp.zeros_like(gx)
    for i, value in enumerate(values + [nothing] * (ROWS - len(values))):
        for a in range(4):
            vals[a, i : i + 1, :] = value[a : a + 1]


def scattered(vals, spread, groups_of, first, count):
    total = None
    for a in range(4):
        both = pair(vals[a])
        chosen = jnp.concatenate(
            [jnp.where(groups_of[a] == first + i, both, 0.0) for i in range(count)], axis=0
        ).astype(jnp.bfloat16)
        term = dot(chosen, spread[a], NT)
        total = term if total is None else total + term
    return jnp.concatenate(
        [unpair(total[2 * ROWS * i : 2 * ROWS * (i + 1)]) for i in range(count)], axis=1
    )


def kernel(
    n_slab, n_grp, *refs,
):
    inputs, (out_ref,), held, rest = refs[:11], refs[11:12], list(refs[12:22]), refs[22:]
    held.insert(6, inputs[6])
    (
        masks_ref, sev_ref, grads_ref, area_ref, disp_ref, stiff_ref, live_ref,
        conn_ref, face_ref, send_rows_ref, seam_rows_ref,
    ) = held
    (
        load_sem,
        near_out, near_in, vals, spread, vals_f, spread_f, send_buf, recv_buf, seam_out, seam_in,
        near_send, near_recv, send_sem, recv_sem, seam_send, seam_recv,
    ) = rest
    loads = {}
    for i in (0, 1, 8, 2, 4, 5, 7, 3, 9, 10):
        loads[i] = pltpu.make_async_copy(inputs[i], held[i], load_sem.at[i])
        loads[i].start()
    f32, bf16, i32 = jnp.float32, jnp.bfloat16, jnp.int32
    s, g = lax.axis_index("slab"), lax.axis_index("grp")
    n = masks_ref.shape[1]
    cap = send_rows_ref.shape[1] // n_slab
    shared = n_slab * cap
    seam = seam_rows_ref.shape[1]
    plies = sev_ref.shape[0]
    groups = n // LO
    beyond = -(-(shared + seam) // LO)
    faces = face_ref.shape[1]
    next_grp = lax.rem(g + 1, n_grp)
    prev_grp = lax.rem(g + n_grp - 1, n_grp)

    barrier = pltpu.get_barrier_semaphore()
    for k in range(1, n_slab):
        pl.semaphore_signal(
            barrier, inc=1, device_id=(lax.rem(s + k, n_slab), g), device_id_type=MESH
        )
    around = (next_grp,) if n_grp == 2 else (next_grp, prev_grp)
    for other in around:
        pl.semaphore_signal(barrier, inc=1, device_id=(s, other), device_id_type=MESH)

    for i in (0, 1, 8):
        loads[i].wait()

    parts = []
    for w in range(plies // 16):
        word = jnp.broadcast_to(masks_ref[w : w + 1, :], (16, n))
        parts.append((word >> lax.broadcasted_iota(i32, (16, n), 0)) & 1)
    damage = jnp.concatenate(parts, axis=0).astype(f32) * sev_ref[...].astype(f32)
    face = jnp.concatenate([face_ref[0:1, :], face_ref[1:2, :]], axis=1)
    onface = (lax.broadcasted_iota(i32, (n, 2 * faces), 0) == face).astype(f32).astype(bf16)
    chosen = dot(damage.astype(bf16), onface, NN).astype(bf16)
    near_out[0] = chosen[:, :faces]
    near_out[1] = chosen[:, faces:]

    pl.semaphore_wait(barrier, n_slab - 1 + len(around))

    to_prev = pltpu.make_async_remote_copy(
        src_ref=near_out.at[0], dst_ref=near_in.at[1], send_sem=near_send.at[0],
        recv_sem=near_recv.at[1], device_id=(lax.max(s - 1, 0), g), device_id_type=MESH,
    )
    to_next = pltpu.make_async_remote_copy(
        src_ref=near_out.at[1], dst_ref=near_in.at[0], send_sem=near_send.at[1],
        recv_sem=near_recv.at[0], device_id=(lax.min(s + 1, n_slab - 1), g), device_id_type=MESH,
    )

    @pl.when(s > 0)
    def _():
        to_prev.start()

    @pl.when(s < n_slab - 1)
    def _():
        to_next.start()

    @pl.when(s == 0)
    def _():
        near_in[0] = jnp.zeros((plies, faces), bf16)

    @pl.when(s == n_slab - 1)
    def _():
        near_in[1] = jnp.zeros((plies, faces), bf16)

    for i in (2, 3, 4, 5, 7, 9, 10):
        loads[i].wait()

    stiff = stiff_ref[...]
    h = 1.0 / plies
    z = -0.5 + h * (lax.broadcasted_iota(i32, (8, plies), 1).astype(f32) + 0.5)
    row8 = lax.broadcasted_iota(i32, (8, plies), 0)
    weights = jnp.concatenate(
        [
            stiff * jnp.where(row8 < 6, h, 5.0 / 6.0 * h),
            stiff * (h * z),
            stiff * (h * z * z + h**3 / 12.0),
        ],
        axis=0,
    )
    w1 = weights.astype(bf16).astype(f32)
    w2 = (weights - w1).astype(bf16).astype(f32)
    w3 = weights - w1 - w2
    wcat = jnp.concatenate([w1, w2, w3], axis=0).astype(bf16)
    total = jnp.sum(weights, axis=1, keepdims=True)
    facing = dot(jnp.ones((16, 2 * faces), bf16), onface, NT)[0:1]
    own = dot(wcat, (damage * (1.0 - 0.5 * facing)).astype(bf16), NN)
    own = total - (own[0:24] + own[24:48] + own[48:72])

    def corners(ref, first, step):
        return jnp.concatenate([ref[first + step * a : first + step * a + 1, :] for a in range(4)], axis=0)

    gx, gy = corners(grads_ref, 0, 2), corners(grads_ref, 1, 2)
    u, v, w, tx, ty, tz = [corners(disp_ref, i, 6) for i in range(6)]
    strain = [
        jnp.sum(t, axis=0, keepdims=True)
        for t in (
            gx * u, gy * v, gy * u + gx * v, gx * ty, -gy * tx, gy * ty - gx * tx,
            gx * w + 0.25 * ty, gy * w - 0.25 * tx, 0.25 * tz - 0.5 * (gx * v - gy * u),
        )
    ]
    column = lax.broadcasted_iota(i32, (1, n), 1)
    area = jnp.where(column < live_ref[0], area_ref[...], 0.0)

    low_row = lax.broadcasted_iota(i32, (LO, n), 0)
    for a in range(4):
        low = conn_ref[a : a + 1, :] & (LO - 1)
        spread[a] = (low_row == low).astype(f32).astype(bf16)

    slots = conn_ref[...]
    picked = jnp.concatenate(
        [gx, gy] + strain + [area, jnp.zeros((6, n), f32)], axis=0
    )
    p1 = picked.astype(bf16).astype(f32)
    p2 = (picked - p1).astype(bf16).astype(f32)
    ints = jnp.concatenate([slots & (LO - 1), slots >> 8], axis=0).astype(f32)
    picked = jnp.concatenate([p1, p2, picked - p1 - p2, ints], axis=0).astype(bf16)
    picked = dot(picked, onface, NN)
    low_f = picked[72:76].astype(i32)
    group_f = picked[76:80].astype(i32)
    picked = picked[0:24] + picked[24:48] + picked[48:72]
    gx_f, gy_f, area_f = picked[0:4], picked[4:8], picked[17:18]
    strain_f = [picked[8 + i : 9 + i] for i in range(9)]
    low_row = lax.broadcasted_iota(i32, (LO, 2 * faces), 0)
    for a in range(4):
        spread_f[a] = (low_row == low_f[a : a + 1]).astype(f32).astype(bf16)

    fill(vals, gx, gy, strain, area * own)
    groups_of = [conn_ref[a : a + 1, :] >> 8 for a in range(4)]
    sums = scattered(vals, spread, groups_of, groups, beyond)

    @pl.when(s > 0)
    def _():
        to_prev.wait_send()
        to_next.wait_recv()

    @pl.when(s < n_slab - 1)
    def _():
        to_next.wait_send()
        to_prev.wait_recv()

    partner = jnp.concatenate([near_in[0], near_in[1]], axis=1)
    other = dot(wcat, partner, NN)
    other = (-0.5 * area_f) * (other[0:24] + other[24:48] + other[48:72])
    fill(vals_f, gx_f, gy_f, strain_f, other)
    groups_f = [group_f[a : a + 1] for a in range(4)]
    sums = sums + scattered(vals_f, spread_f, groups_f, groups, beyond)

    row_of = lax.broadcasted_iota(i32, (ROWS, 128), 0)
    for b in range(shared // 128):
        ids = send_rows_ref[:, 128 * b : 128 * (b + 1)].astype(f32)
        block = jnp.where(row_of == ID_ROW, ids, sums[:, 128 * b : 128 * (b + 1)])
        block = jnp.concatenate([block, jnp.zeros((128 - ROWS, 128), f32)], axis=0).T
        send_buf[pl.ds(b * (128 // cap), 128 // cap)] = block.reshape(128 // cap, cap, 128)
    copies = []
    for k in range(1, n_slab):
        to = lax.rem(s + k, n_slab)
        copies.append(
            pltpu.make_async_remote_copy(
                src_ref=send_buf.at[to], dst_ref=recv_buf.at[s], send_sem=send_sem.at[k],
                recv_sem=recv_sem.at[k], device_id=(to, g), device_id_type=MESH,
            )
        )
        copies[-1].start()
    seam_out[...] = jnp.where(
        row_of == ID_ROW, seam_rows_ref[...].astype(f32), sums[:, shared : shared + seam]
    )
    copies.append(
        pltpu.make_async_remote_copy(
            src_ref=seam_out, dst_ref=seam_in, send_sem=seam_send, recv_sem=seam_recv,
            device_id=(s, next_grp), device_id_type=MESH,
        )
    )
    copies[-1].start()
    recv_buf[s] = send_buf[s]

    owned = scattered(vals, spread, groups_of, 0, groups)
    owned = owned + scattered(vals_f, spread_f, groups_f, 0, groups)

    for copy in copies:
        copy.wait()

    row_lane = lax.broadcasted_iota(i32, (128, n), 1)
    for b in range(shared // 128 + 1):
        if b < shared // 128:
            across = recv_buf[pl.ds(b * (128 // cap), 128 // cap)].reshape(128, 128)
            block = across.T[:ROWS]
        else:
            block = seam_in[...]
            across = jnp.concatenate([block, jnp.zeros((128 - ROWS, 128), f32)], axis=0).T
        ids = across[:, ID_ROW : ID_ROW + 1].astype(i32)
        onto = (row_lane == ids).astype(f32).astype(bf16)
        owned = owned + unpair(dot(pair(block).astype(bf16), onto, NN))

    out_ref[...] = owned


def expand(rows_ref, out_ref):
    zero = jnp.zeros((1, rows_ref.shape[1]), jnp.float32)
    for j in range(6):
        for k in range(6):
            at = PAIRS.get((min(j, k), max(j, k)))
            row = 6 * j + k
            out_ref[row : row + 1, :] = zero if at is None else rows_ref[at : at + 1, :]
    for j in range(6):
        out_ref[36 + j : 37 + j, :] = rows_ref[16 + j : 17 + j, :]


def on_device(
    n_slab, n_grp, ply_masks, severity, shape_grads, element_area, displacement, ply_stiffness,
    live_counts, connectivity, interface_slots, send_rows, seam_rows,
):
    f32, bf16 = jnp.float32, jnp.bfloat16
    n = ply_masks.shape[1]
    plies = severity.shape[0]
    cap = send_rows.shape[0] // n_slab
    faces = interface_slots.shape[1]
    seam = seam_rows.shape[0]
    arrays = (
        ply_masks, severity, shape_grads, element_area[None], displacement, ply_stiffness,
        live_counts, connectivity, interface_slots, send_rows[None], seam_rows[None],
    )
    hbm = pl.BlockSpec(memory_space=pltpu.HBM)
    held = [pltpu.VMEM(a.shape, a.dtype) for a in arrays]
    held = held[:6] + held[7:]
    rows = pl.pallas_call(
        functools.partial(kernel, n_slab, n_grp),
        out_shape=jax.ShapeDtypeStruct((ROWS, n), f32),
        in_specs=[hbm] * 6 + [pl.BlockSpec(memory_space=pltpu.SMEM)] + [hbm] * 4,
        out_specs=pl.BlockSpec(memory_space=pltpu.VMEM),
        scratch_shapes=held + [
            pltpu.SemaphoreType.DMA((len(arrays),)),
            pltpu.VMEM((2, plies, faces), bf16),
            pltpu.VMEM((2, plies, faces), bf16),
            pltpu.VMEM((4, ROWS, n), f32),
            pltpu.VMEM((4, LO, n), bf16),
            pltpu.VMEM((4, ROWS, 2 * faces), f32),
            pltpu.VMEM((4, LO, 2 * faces), bf16),
            pltpu.VMEM((n_slab, cap, 128), f32),
            pltpu.VMEM((n_slab, cap, 128), f32),
            pltpu.VMEM((ROWS, seam), f32),
            pltpu.VMEM((ROWS, seam), f32),
            pltpu.SemaphoreType.DMA((2,)),
            pltpu.SemaphoreType.DMA((2,)),
            pltpu.SemaphoreType.DMA((n_slab,)),
            pltpu.SemaphoreType.DMA((n_slab,)),
            pltpu.SemaphoreType.DMA,
            pltpu.SemaphoreType.DMA,
        ],
        compiler_params=pltpu.CompilerParams(
            collective_id=0, has_side_effects=True, vmem_limit_bytes=64 * 1024 * 1024
        ),
    )(*arrays)
    vmem = pl.BlockSpec(memory_space=pltpu.VMEM)
    return pl.pallas_call(
        expand, out_shape=jax.ShapeDtypeStruct((42, n), f32), in_specs=[vmem], out_specs=vmem
    )(rows)


def solution(mesh):
    both = ("slab", "grp")
    in_specs = (
        P(None, both), P(None, both), P(None, both), P(both), P(None, both), P(), P(both),
        P(None, both), P(None, both), P(both), P(both),
    )
    return jax.shard_map(
        functools.partial(on_device, mesh.shape["slab"], mesh.shape["grp"]),
        mesh=mesh, in_specs=in_specs, out_specs=P(None, both), check_vma=False,
    )
```

time: 19.4 us -> 18.1 us (0.933)
  local copies, waits for them, and re-layouts: 1.62 us -> 0 us
  Pallas kernels: 16.9 us -> 17.2 us
    unnamed x1 -> x0, local copies, waits for them, and re-layouts: 1.62 us -> none
    pallas_call x0 -> x1, Pallas kernels: none -> 1.6 us  [on_device(): pl.pallas_call(expand, out_shape=jax.ShapeDtypeStruct((42, n), f32), in_s...]
    pallas_call x1, Pallas kernels: 16.9 us -> 15.6 us  [on_device(): pl.pallas_call(functools.partial(kernel, n_slab, n_grp), out_shape=jax.Sh...]
where the time goes in v3:
time: 18.1 us; the launch traced here: 17.8 us
  Pallas kernels  17.2 us (95%)
  between operations  0.66 us (4%)
    pallas_call x1, Pallas kernels, on_device(): pl.pallas_call(functools.partial(kernel, n_slab, n_grp), out_shape=jax.Sh...  15.6 us
    pallas_call x1, Pallas kernels, on_device(): pl.pallas_call(expand, out_shape=jax.ShapeDtypeStruct((42, n), f32), in_s...  1.6 us

profile of v3, /device:TPU:0, one launch (start us, length us, event | category | flops | bytes accessed | tf_op | source)
XLA Modules:
  0.0 17.8 jit_solution(4756062716300851142)
XLA Ops:
  0.7 15.6 %shard_map.109.rows_ref = f32[24,1024]{1,0:T(8,128)} custom-call(s32[3,1024]{1,0:T(4,128)} %refs_0_.1, bf16[48,1024]{1,0:T(8,128)(2,1)} %refs_1_.1, f32[8,1024]{1,0:T(8,128)} %refs_2_.1, f32[1,1024]{1,0:T(1,128)} %bitcast.3, f32[24,1024]{1,0:T(8,128)} %refs_4_.1, f32[8,48]{1,0:T(8,128)} %refs_5_.1, s32[1]{0:T(128)S(6)} %copy.12.refs_6_, s32[4,1024]{1,0:T(4,128)} %refs_7_.1, ...), custom_call_target="tpu_custom_call" | custom-call | tf_op jit(solution)/shard_map/pallas_call | solution.py:344
  16.2 1.6 %shard_map.110 = f32[42,1024]{1,0:T(8,128)} custom-call(f32[24,1024]{1,0:T(8,128)} %shard_map.109.rows_ref), custom_call_target="tpu_custom_call" | custom-call | tf_op jit(solution)/shard_map/pallas_call | solution.py:373

commit v4 on v3

--- a/solution.py
+++ b/solution.py
@@ -111,11 +111,11 @@
     ) = held
     (
         load_sem,
-        near_out, near_in, vals, spread, vals_f, spread_f, send_buf, recv_buf, seam_out, seam_in,
+        near_out, near_in, vals, spread, vals_f, spread_f, onface, send_buf, recv_buf, seam_out, seam_in,
         near_send, near_recv, send_sem, recv_sem, seam_send, seam_recv,
     ) = rest
     loads = {}
-    for i in (0, 1, 8, 2, 4, 5, 7, 3, 9, 10):
+    for i in (8, 1, 0, 2, 4, 5, 7, 3, 9, 10):
         loads[i] = pltpu.make_async_copy(inputs[i], held[i], load_sem.at[i])
         loads[i].start()
     f32, bf16, i32 = jnp.float32, jnp.bfloat16, jnp.int32
@@ -140,7 +140,10 @@
     for other in around:
         pl.semaphore_signal(barrier, inc=1, device_id=(s, other), device_id_type=MESH)
 
-    for i in (0, 1, 8):
+    loads[8].wait()
+    face = jnp.concatenate([face_ref[0:1, :], face_ref[1:2, :]], axis=1)
+    onface[...] = (lax.broadcasted_iota(i32, (n, 2 * faces), 0) == face).astype(f32).astype(bf16)
+    for i in (0, 1):
         loads[i].wait()
 
     parts = []
@@ -148,9 +151,7 @@
         word = jnp.broadcast_to(masks_ref[w : w + 1, :], (16, n))
         parts.append((word >> lax.broadcasted_iota(i32, (16, n), 0)) & 1)
     damage = jnp.concatenate(parts, axis=0).astype(f32) * sev_ref[...].astype(f32)
-    face = jnp.concatenate([face_ref[0:1, :], face_ref[1:2, :]], axis=1)
-    onface = (lax.broadcasted_iota(i32, (n, 2 * faces), 0) == face).astype(f32).astype(bf16)
-    chosen = dot(damage.astype(bf16), onface, NN).astype(bf16)
+    chosen = dot(damage.astype(bf16), onface[...], NN).astype(bf16)
     near_out[0] = chosen[:, :faces]
     near_out[1] = chosen[:, faces:]
 
@@ -201,7 +202,7 @@
     w3 = weights - w1 - w2
     wcat = jnp.concatenate([w1, w2, w3], axis=0).astype(bf16)
     total = jnp.sum(weights, axis=1, keepdims=True)
-    facing = dot(jnp.ones((16, 2 * faces), bf16), onface, NT)[0:1]
+    facing = dot(jnp.ones((16, 2 * faces), bf16), onface[...], NT)[0:1]
     own = dot(wcat, (damage * (1.0 - 0.5 * facing)).astype(bf16), NN)
     own = total - (own[0:24] + own[24:48] + own[48:72])
 
@@ -233,7 +234,7 @@
     p2 = (picked - p1).astype(bf16).astype(f32)
     ints = jnp.concatenate([slots & (LO - 1), slots >> 8], axis=0).astype(f32)
     picked = jnp.concatenate([p1, p2, picked - p1 - p2, ints], axis=0).astype(bf16)
-    picked = dot(picked, onface, NN)
+    picked = dot(picked, onface[...], NN)
     low_f = picked[72:76].astype(i32)
     group_f = picked[76:80].astype(i32)
     picked = picked[0:24] + picked[24:48] + picked[48:72]
@@ -299,17 +300,18 @@
         copy.wait()
 
     row_lane = lax.broadcasted_iota(i32, (128, n), 1)
+    blocks, onto = [], []
     for b in range(shared // 128 + 1):
         if b < shared // 128:
             across = recv_buf[pl.ds(b * (128 // cap), 128 // cap)].reshape(128, 128)
-            block = across.T[:ROWS]
+            blocks.append(across.T[:ROWS])
         else:
-            block = seam_in[...]
-            across = jnp.concatenate([block, jnp.zeros((128 - ROWS, 128), f32)], axis=0).T
+            blocks.append(seam_in[...])
+            across = jnp.concatenate([blocks[-1], jnp.zeros((128 - ROWS, 128), f32)], axis=0).T
         ids = across[:, ID_ROW : ID_ROW + 1].astype(i32)
-        onto = (row_lane == ids).astype(f32).astype(bf16)
-        owned = owned + unpair(dot(pair(block).astype(bf16), onto, NN))
-
+        onto.append((row_lane == ids).astype(f32).astype(bf16))
+    blocks = pair(jnp.concatenate(blocks, axis=1)).astype(bf16)
+    owned = owned + unpair(dot(blocks, jnp.concatenate(onto, axis=0), NN))
     out_ref[...] = owned
 
 
@@ -354,6 +356,7 @@
             pltpu.VMEM((4, LO, n), bf16),
             pltpu.VMEM((4, ROWS, 2 * faces), f32),
             pltpu.VMEM((4, LO, 2 * faces), bf16),
+            pltpu.VMEM((n, 2 * faces), bf16),
             pltpu.VMEM((n_slab, cap, 128), f32),
             pltpu.VMEM((n_slab, cap, 128), f32),
             pltpu.VMEM((ROWS, seam), f32),

time: 18.1 us -> 18.1 us (level)
  no operation moved by 1% of the time
where the time goes in v4:
time: 18.1 us; the launch traced here: 17.9 us
  Pallas kernels  17.2 us (95%)
  between operations  0.66 us (4%)
    pallas_call x1, Pallas kernels, on_device(): pl.pallas_call(functools.partial(kernel, n_slab, n_grp), out_shape=jax.Sh...  15.6 us
    pallas_call x1, Pallas kernels, on_device(): pl.pallas_call(expand, out_shape=jax.ShapeDtypeStruct((42, n), f32), in_s...  1.6 us

profile of v4, /device:TPU:0, one launch (start us, length us, event | category | flops | bytes accessed | tf_op | source)
XLA Modules:
  0.0 17.9 jit_solution(11388000726959240317)
XLA Ops:
  0.7 15.6 %shard_map.109.rows_ref = f32[24,1024]{1,0:T(8,128)} custom-call(s32[3,1024]{1,0:T(4,128)} %refs_0_.1, bf16[48,1024]{1,0:T(8,128)(2,1)} %refs_1_.1, f32[8,1024]{1,0:T(8,128)} %refs_2_.1, f32[1,1024]{1,0:T(1,128)} %bitcast.3, f32[24,1024]{1,0:T(8,128)} %refs_4_.1, f32[8,48]{1,0:T(8,128)} %refs_5_.1, s32[1]{0:T(128)S(6)} %copy.12.refs_6_, s32[4,1024]{1,0:T(4,128)} %refs_7_.1, ...), custom_call_target="tpu_custom_call" | custom-call | tf_op jit(solution)/shard_map/pallas_call | solution.py:346
  16.3 1.6 %shard_map.110 = f32[42,1024]{1,0:T(8,128)} custom-call(f32[24,1024]{1,0:T(8,128)} %shard_map.109.rows_ref), custom_call_target="tpu_custom_call" | custom-call | tf_op jit(solution)/shard_map/pallas_call | solution.py:376
